TPU v7x, 1024 devices: a whole 4x4x32 slice. The times are simulated.
1024 devices in a mesh: dp: 16 (over x, y), expert: 64 (over z, core).
Axes of the slice: x: 4, y: 4, z: 32, core: 2. Of those that a mesh axis runs over, the one named last changes fastest.
Arguments:
- tokens: bfloat16 [8192, 6144], P('expert', 'dp'), may hold values from -6 to 6
- cotangent: bfloat16 [8192, 6144], P('expert', 'dp'), may hold values from -6 to 6
- expert_ids: int32 [8192, 8], P('expert'), may hold values from 0 to 127, all different within a row; in each aligned block of 128 rows (0 to 127, 128 to 255, ...) at most 10 rows name the same one
- route_weights: float32 [8192, 8], P('expert'), may hold values from 0.1 to 1
- up_weight: bfloat16 [128, 6144, 1024], P('expert', 'dp'), may hold values from -0.078125 to 0.078125
- down_weight: bfloat16 [128, 1024, 6144], P('expert', None, 'dp'), may hold values from -0.1875 to 0.1875
Outputs:
- critic_out: bfloat16 [8192, 6144], P('expert', 'dp')
- token_grad: bfloat16 [8192, 6144], P('expert', 'dp')
Inputs may be any that keep to these rules, and one draw needn't show every extreme that they name: `expert_ids`: each row names 8 different experts. Within every aligned block of 128 rows no expert is named by more than 10 rows, and in some block one expert is named by exactly 10 rows.
All inputs are finite; a program needn't handle non-finite values.
Results may differ from a plain program's by a relative error of at most 0.025.
Values may be sent and summed in bfloat16 or wider, within the bound.
A program may use at most 64 MiB of HBM per device.

v0:
```python
import jax
import jax.numpy as jnp
from jax import lax
from jax.sharding import PartitionSpec as P


def silu_slope(pre):
    sigmoid_part = jax.nn.sigmoid(pre)
    return sigmoid_part * (1.0 + pre * (1.0 - sigmoid_part))


def partial_terms(x_rows, dy_rows, up_weight, down_weight, groups):
    width = x_rows.shape[-1]
    x_three = x_rows.reshape(-1, groups, width)
    dy_three = dy_rows.reshape(-1, groups, width)
    pre = jnp.einsum("rld,ldf->rlf", x_three, up_weight, preferred_element_type=jnp.float32)
    grad_hidden = jnp.einsum(
        "rld,lfd->rlf", dy_three, down_weight, preferred_element_type=jnp.float32
    )
    units = pre.shape[-1]
    return jnp.stack([pre.reshape(-1, units), grad_hidden.reshape(-1, units)], axis=1)


def activate(shares):
    pre = shares[:, 0]
    grad_hidden = shares[:, 1]
    hidden = jax.nn.silu(pre).astype(jnp.bfloat16)
    grad_pre = (grad_hidden * silu_slope(pre)).astype(jnp.bfloat16)
    return jnp.stack([hidden, grad_pre], axis=1)


def project_back(stacked, up_weight, down_weight, groups):
    units = stacked.shape[-1]
    four = stacked.reshape(-1, groups, 2, units)
    out = jnp.einsum("rlf,lfd->rld", four[:, :, 0], down_weight, preferred_element_type=jnp.float32)
    back = jnp.einsum("rlf,ldf->rld", four[:, :, 1], up_weight, preferred_element_type=jnp.float32)
    width = out.shape[-1]
    return jnp.stack([out.reshape(-1, width), back.reshape(-1, width)], axis=1).astype(jnp.bfloat16)


def local(tokens, cotangent, expert_ids, route_weights, up_weight, down_weight):
    tok_rows, picks_per = expert_ids.shape
    groups = up_weight.shape[0]
    width = tokens.shape[1]
    peers = lax.axis_size("expert")
    experts = groups * peers
    capacity = max(2, 5 * tok_rows * picks_per // (4 * experts))
    slots = experts * capacity
    flat = expert_ids.reshape(-1)
    onehot = (flat[:, None] == jnp.arange(experts, dtype=jnp.int32)[None, :]).astype(jnp.int32)
    earlier = jnp.cumsum(onehot, axis=0) - onehot
    place = jnp.sum(earlier * onehot, axis=1)
    slot_ids = (flat // groups * capacity + place) * groups + flat % groups
    match = (jnp.arange(slots, dtype=jnp.int32)[:, None] == slot_ids[None, :]).reshape(
        slots, tok_rows, picks_per
    )
    dispatch_table = jnp.sum(match.astype(jnp.int32), axis=2).astype(jnp.bfloat16)
    slot_weight = jnp.sum(match.astype(jnp.float32) * route_weights[None, :, :], axis=(1, 2))
    x_send = jnp.dot(dispatch_table, tokens, preferred_element_type=jnp.float32).astype(
        jnp.bfloat16
    )
    dy_plain = jnp.dot(dispatch_table, cotangent, preferred_element_type=jnp.float32)
    dy_send = (slot_weight[:, None] * dy_plain).astype(jnp.bfloat16)
    x_recv, dy_recv = (
        lax.all_to_all(
            x_send.reshape(peers, capacity * groups, width),
            "expert",
            split_axis=0,
            concat_axis=0,
            tiled=True,
        ),
        lax.all_to_all(
            dy_send.reshape(peers, capacity * groups, width),
            "expert",
            split_axis=0,
            concat_axis=0,
            tiled=True,
        ),
    )
    total_rows = peers * capacity * groups
    x_recv = x_recv.reshape(total_rows, width)
    dy_recv = dy_recv.reshape(total_rows, width)
    terms = partial_terms(x_recv, dy_recv, up_weight, down_weight, groups)
    shares = lax.psum_scatter(
        terms.astype(jnp.bfloat16), "dp", scatter_dimension=2, tiled=True
    ).astype(jnp.float32)
    stacked = activate(shares)
    whole = lax.all_gather(stacked, "dp", axis=2, tiled=True)
    returned = project_back(whole, up_weight, down_weight, groups)
    arrived = lax.all_to_all(
        returned.reshape(peers, capacity * groups, 2, width),
        "expert",
        split_axis=0,
        concat_axis=0,
        tiled=True,
    )
    arrived = arrived.reshape(slots, 2, width)
    picked = arrived[slot_ids].reshape(tok_rows, picks_per, 2, width).astype(jnp.float32)
    critic_out = jnp.sum(route_weights[:, :, None] * picked[:, :, 0], axis=1).astype(jnp.bfloat16)
    token_grad = jnp.sum(picked[:, :, 1], axis=1).astype(jnp.bfloat16)
    return (critic_out, token_grad)


def solution(mesh):
    in_specs = (
        P("expert", "dp"),
        P("expert", "dp"),
        P("expert", None),
        P("expert", None),
        P("expert", "dp", None),
        P("expert", None, "dp"),
    )
    out_specs = (P("expert", "dp"), P("expert", "dp"))
    return jax.shard_map(local, mesh=mesh, in_specs=in_specs, out_specs=out_specs, check_vma=False)
```

profile of v0, /device:TPU:1, one launch (start us, length us, event | category | flops | bytes accessed | tf_op | source)
XLA Modules:
  0.0 881.0 jit_solution(12648516329262498741)
XLA Ops:
  7.2 0.9 copy.77
  8.3 0.4 copy-done.1
  9.2 0.4 fusion.11
  9.8 6.7 convert_reduce_fusion
  16.5 0.4 convolution_convert_fusion
  16.9 1.1 reshape.227
  18.0 30.4 %all-to-all-start = ((bf16[64,20,384]{2,1,0:T(8,128)(2,1)}), bf16[64,20,384]{2,1,0:T(8,128)(2,1)S(1)}, u32[]{:S(2)}, u32[]{:S(2)}) async-start(bf16[64,20,384]{2,1,0:T(8,128)(2,1)} %reshape.227), calls=%async_computation | async-start | bytes 2359296 | tf_op jit(solution)/shard_map/all_to_all | solution.py:65
  48.4 9.6 %select_reduce_fusion = f32[1280]{0:T(1024)S(1)} fusion(f32[128,8]{0,1:T(8,128)S(1)} %copy-done.6, s32[128,8]{0,1:T(8,128)S(1)} %fusion.22), kind=kLoop, calls=%fused_computation.2 | loop fusion | flops 3930880 | bytes 13312 | tf_op jit(solution)/shard_map/reduce_sum | solution.py:58
  58.0 1.4 fusion
  59.5 2.2 reshape.228
  61.6 106.3 %all-to-all-done = bf16[64,20,384]{2,1,0:T(8,128)(2,1)S(1)} async-done(((bf16[64,20,384]{2,1,0:T(8,128)(2,1)}), bf16[64,20,384]{2,1,0:T(8,128)(2,1)S(1)}, u32[]{:S(2)}, u32[]{:S(2)}) %all-to-all-start) | async-done | bytes 983072 | tf_op jit(solution)/shard_map/all_to_all | solution.py:65
  167.9 7.8 all-to-all-start.1
  175.7 0.5 all-reduce.3.cloned.1.call-start
  176.2 1.5 reshape_reshape.6
  177.7 3.2 convert_bitcast_fusion.1
  181.0 4.2 copy.83
  185.2 5.1 stack_reshape.10
  190.3 104.7 %all-to-all-done.1 = bf16[64,20,384]{2,1,0:T(8,128)(2,1)} async-done(((bf16[64,20,384]{2,1,0:T(8,128)(2,1)}), bf16[64,20,384]{2,1,0:T(8,128)(2,1)}, u32[]{:S(2)}, u32[]{:S(2)}) %all-to-all-start.1) | async-done | bytes 983072 | tf_op jit(solution)/shard_map/all_to_all | solution.py:72
  295.0 2.6 reshape_reshape.7
  297.6 1.6 convert_bitcast_fusion
  299.1 4.2 copy.85
  303.3 5.1 stack_reshape.11
  308.4 5.3 pad_maximum_fusion
  313.8 13.8 %copy.86 = bf16[1280,2,1024]{0,1,2:T(2,128)(2,1)} copy(bf16[1280,2,1024]{2,0,1:T(8,128)(2,1)} %pad_maximum_fusion) | data formatting | bytes 10485760 | tf_op jit(solution)/shard_map/stack | solution.py:21
  327.5 0.2 all-gather.2.cloned.1.call-start
  327.8 1.3 dynamic-slice
  329.7 166.3 %all-reduce.3.cloned.1.call-done = bf16[1280,2,1024]{0,1,2:T(2,128)(2,1)} async-done(((bf16[1280,2,1024]{0,1,2:T(2,128)(2,1)}), bf16[1280,2,1024]{0,1,2:T(2,128)(2,1)}) %all-reduce.3.cloned.1.call-update) | async-done | bytes 5242896
  496.0 1.2 constant_dynamic-slice_fusion
  497.5 1.1 copy.88
  498.6 94.7 %all-gather.2.cloned.1.call-done = bf16[1280,2,1024]{0,1,2:T(2,128)(2,1)} async-done(((bf16[1280,2,64]{0,1,2:T(2,128)(2,1)}), bf16[1280,2,1024]{0,1,2:T(2,128)(2,1)}) %all-gather.2.cloned.1.call-update) | async-done | bytes 5242896 | tf_op jit(solution)/shard_map/all_gather | solution.py:88
  593.3 19.6 %copy.89 = bf16[1280,2,1024]{2,1,0:T(2,128)(2,1)} copy(bf16[1280,2,1024]{0,1,2:T(2,128)(2,1)} %all-gather.2.cloned.1.call-done) | data formatting | bytes 10485760 | tf_op jit(solution)/shard_map/all_gather | solution.py:88
  612.9 11.7 %fusion.27 = (bf16[640,2,1,1024]{3,2,1,0:T(2,128)(2,1)S(1)}, bf16[640,2,1,1024]{3,2,1,0:T(2,128)(2,1)}) fusion(bf16[640,2,2,1024]{3,2,1,0:T(2,128)(2,1)} %bitcast.50), kind=kLoop, calls=%fused_computation.66 | loop fusion | bytes 10485760 | tf_op jit(solution)/shard_map/slice | solution.py:35
  624.6 1.6 fusion.7
  626.3 2.0 copy.91
  628.3 2.6 stack.18
  630.9 4.7 fusion.6
  635.6 2.0 copy.93
  637.6 3.3 stack.19
  640.9 1.7 pad_maximum_fusion.1
  642.6 3.3 copy.94
  645.9 24.0 %all-to-all-start.2 = ((bf16[64,20,2,384]{3,2,1,0:T(2,128)(2,1)}), bf16[64,20,2,384]{3,2,1,0:T(2,128)(2,1)S(1)}, u32[]{:S(2)}, u32[]{:S(2)}) async-start(bf16[64,20,2,384]{3,2,1,0:T(2,128)(2,1)} %copy.94), calls=%async_computation.2 | async-start | bytes 3932160 | tf_op jit(solution)/shard_map/all_to_all | solution.py:90
  669.9 0.9 reshape.231
  670.8 0.7 copy.76
  671.6 184.9 %all-to-all-done.2 = bf16[64,20,2,384]{3,2,1,0:T(2,128)(2,1)S(1)} async-done(((bf16[64,20,2,384]{3,2,1,0:T(2,128)(2,1)}), bf16[64,20,2,384]{3,2,1,0:T(2,128)(2,1)S(1)}, u32[]{:S(2)}, u32[]{:S(2)}) %all-to-all-start.2) | async-done | bytes 1966112 | tf_op jit(solution)/shard_map/all_to_all | solution.py:90
  856.5 9.6 %gather_fusion = bf16[1024,2,384]{2,1,0:T(2,128)(2,1)} fusion(bf16[1280,2,384]{2,1,0:T(2,128)(2,1)S(1)} %bitcast.51, s32[1024]{0:T(1024)S(1)} %broadcast_clamp_fusion), kind=kCustom, calls=%fused_computation | custom fusion | bytes 3149824 | tf_op jit(solution)/shard_map/gather | solution.py:98
  866.2 2.5 bitcast_convert_fusion
  868.7 4.2 slice_reduce_fusion
  872.8 1.1 fusion.3
  (32 shorter events, 1.2 us)
Async XLA Ops:
  7.2 290.4 %copy-start = (bf16[2,1024,384]{2,1,0:T(8,128)(2,1)S(1)}, bf16[2,1024,384]{2,1,0:T(8,128)(2,1)}, u32[]{:S(2)}) copy-start(bf16[2,1024,384]{2,1,0:T(8,128)(2,1)} %param.11) | copy-start | bytes 4718596
  7.2 2.6 copy-start.5
  7.2 9.3 %copy-start.3 = (bf16[128,384]{1,0:T(8,128)(2,1)S(1)}, bf16[128,384]{1,0:T(8,128)(2,1)}, u32[]{:S(2)}) copy-start(bf16[128,384]{1,0:T(8,128)(2,1)} %param.6) | copy-start | bytes 294916
  8.1 0.6 copy-start.1
  16.9 31.6 %copy-start.6 = (f32[128,8]{0,1:T(8,128)S(1)}, f32[128,8]{0,1:T(8,128)}, u32[]{:S(2)}) copy-start(f32[128,8]{0,1:T(8,128)} %param.9) | copy-start | bytes 12292
  16.9 41.2 %copy-start.4 = (bf16[128,384]{1,0:T(8,128)(2,1)S(1)}, bf16[128,384]{1,0:T(8,128)(2,1)}, u32[]{:S(2)}) copy-start(bf16[128,384]{1,0:T(8,128)(2,1)} %param.7) | copy-start | bytes 294916
  18.0 149.8 %all-to-all-start = ((bf16[64,20,384]{2,1,0:T(8,128)(2,1)}), bf16[64,20,384]{2,1,0:T(8,128)(2,1)S(1)}, u32[]{:S(2)}, u32[]{:S(2)}) async-start(bf16[64,20,384]{2,1,0:T(8,128)(2,1)} %reshape.227), calls=%async_computation | async-start | bytes 2359296 | tf_op jit(solution)/shard_map/all_to_all | solution.py:65
  167.9 127.1 %all-to-all-start.1 = ((bf16[64,20,384]{2,1,0:T(8,128)(2,1)}), bf16[64,20,384]{2,1,0:T(8,128)(2,1)}, u32[]{:S(2)}, u32[]{:S(2)}) async-start(bf16[64,20,384]{2,1,0:T(8,128)(2,1)} %reshape.228), calls=%async_computation.1 | async-start | bytes 2359296 | tf_op jit(solution)/shard_map/all_to_all | solution.py:72
  175.7 320.4 %all-reduce.3.cloned.1.call-start = ((), (), s32[]{:S(2)}) async-start(), calls=%async_computation.4 | async-start | bytes 10485760
  327.5 265.8 %all-gather.2.cloned.1.call-start = ((), (), s32[]{:S(2)}) async-start(), calls=%async_computation.3 | async-start | bytes 5570560 | tf_op jit(solution)/shard_map/all_gather | solution.py:88
  645.9 210.6 %all-to-all-start.2 = ((bf16[64,20,2,384]{3,2,1,0:T(2,128)(2,1)}), bf16[64,20,2,384]{3,2,1,0:T(2,128)(2,1)S(1)}, u32[]{:S(2)}, u32[]{:S(2)}) async-start(bf16[64,20,2,384]{3,2,1,0:T(2,128)(2,1)} %copy.94), calls=%async_computation.2 | async-start | bytes 3932160 | tf_op jit(solution)/shard_map/all_to_all | solution.py:90
  868.6 4.2 copy-start.2
Sparse Core Ops, SparseCore 0:
  327.7 168.3 all-reduce.2
  501.0 92.2 all-gather.1
where the time goes:
time: 892 us; the launch traced here: 881 us
  waiting for transfers between devices  657 us (74%)
  local copies, waits for them, and re-layouts  101 us (11%)
  starting transfers between devices  62.9 us (7%)
  other arithmetic  32 us (4%)
  between operations  15.2 us (2%)
  matrix products  13 us (1%)
    all_to_all x1, waiting for transfers between devices, local(): lax.all_to_all(returned.reshape(peers, capacity * groups, 2, width), 'exp...  185 us
    unnamed x3, waiting for transfers between devices  166 us
    all_to_all x1, waiting for transfers between devices, local(): lax.all_to_all(x_send.reshape(peers, capacity * groups, width), 'expert',...  106 us
    all_to_all x1, waiting for transfers between devices, local(): lax.all_to_all(dy_send.reshape(peers, capacity * groups, width), 'expert'...  105 us
    all_gather x1, waiting for transfers between devices, local(): whole = lax.all_gather(stacked, 'dp', axis=2, tiled=True)  94.7 us
    all_to_all x1, starting transfers between devices, local(): lax.all_to_all(x_send.reshape(peers, capacity * groups, width), 'expert',...  30.4 us
    another operation x3, local copies, waits for them, and re-layouts, partial_terms(): jnp.stack([pre.reshape(-1, units), grad_hidden.reshape(-1, units)], axis=1)  24 us
    all_to_all x1, starting transfers between devices, local(): lax.all_to_all(returned.reshape(peers, capacity * groups, 2, width), 'exp...  24 us
  transfers between devices with their start and end apart: 5, of which 5 were waited for; matrix products, arithmetic and copies ran while one was open for 3% of the time, Pallas kernels for 0%

commit v1 on v0

v1 whole, which is shorter than its diff:
```python
import functools

import jax
import jax.numpy as jnp
from jax import lax
from jax.experimental import pallas as pl
from jax.experimental.pallas import tpu as pltpu
from jax.sharding import PartitionSpec as P

MESH = pl.DeviceIdType.MESH
F32 = jnp.float32
BF16 = jnp.bfloat16
SIDE = 4
CAP = 10


def dot(a, b, ca, cb, precision=None):
    return lax.dot_general(
        a, b, (((ca,), (cb,)), ((), ())), precision=precision, preferred_element_type=F32
    )


def kernel(
    n_chips,
    x_ref, dy_ref, meta_ref, up_hbm, down_hbm, critic_ref, grad_ref,
    up, down, gx, gc, gm, terms, a1, a2, s1, b1, b2, acts, table, slot_w, rx, pc,
    w_sem, ag_send, ag_recv, pair_send, pair_recv, ex_send, ex_recv,
    rs_send, rs_recv, back_send, back_recv,
):
    reach = n_chips // 2
    chunks = reach // 2
    rounds = chunks // 2
    dp, ex = lax.axis_index("dp"), lax.axis_index("expert")
    x, y = lax.div(dp, SIDE), lax.rem(dp, SIDE)
    z, core = lax.div(ex, 2), lax.rem(ex, 2)
    z_up = (dp, lax.rem(z + 1, n_chips) * 2 + core)
    z_down = (dp, lax.rem(z + n_chips - 1, n_chips) * 2 + core)
    partner = (dp, z * 2 + 1 - core)

    def along(axis, step):
        if axis == 0:
            return (lax.rem(x + step, SIDE) * SIDE + y, ex)
        return (x * SIDE + lax.rem(y + step, SIDE), ex)

    weights_in = (
        pltpu.make_async_copy(up_hbm, up, w_sem.at[0]),
        pltpu.make_async_copy(down_hbm, down, w_sem.at[1]),
    )
    for copy in weights_in:
        copy.start()

    barrier = pltpu.get_barrier_semaphore()
    others = (z_up, z_down, partner, along(0, 1), along(0, 3), along(1, 1), along(1, 3))
    for device in others:
        pl.semaphore_signal(barrier, inc=1, device_id=device, device_id_type=MESH)
    pl.semaphore_wait(barrier, len(others))

    def remote(src, dst, send, recv, device):
        return pltpu.make_async_remote_copy(
            src_ref=src, dst_ref=dst, send_sem=send, recv_sem=recv,
            device_id=device, device_id_type=MESH,
        )

    def pair_no(distance, way):
        return (distance - 1) * 2 + way

    gathered = (gx, gc, gm)
    own = pair_no(reach, 1)

    def to_chip(stream, src, dst, device):
        g = gathered[stream]
        return remote(
            g.at[2 * src], g.at[2 * dst], ag_send.at[stream, dst], ag_recv.at[stream, dst], device
        )

    def to_partner(stream, no):
        g = gathered[stream]
        return remote(
            g.at[2 * no], g.at[2 * no + 1], pair_send.at[stream, no], pair_recv.at[stream, no],
            partner,
        )

    gx[2 * own] = x_ref[...]
    gc[2 * own] = dy_ref[...]
    gm[2 * own] = meta_ref[...]
    for stream in range(3):
        to_chip(stream, own, pair_no(1, 0), z_up).start()
        to_chip(stream, own, pair_no(1, 1), z_down).start()
    for stream in range(3):
        to_partner(stream, own).start()

    def gather_tick(distance):
        for stream in range(3):
            for way, device in ((0, z_up), (1, z_down)):
                no = pair_no(distance, way)

                def arrive():
                    to_chip(stream, no, no, device).wait_recv()

                    @pl.when(distance < reach - way)
                    def _():
                        to_chip(stream, no, no + 2, device).start()

                    to_partner(stream, no).start()

                if way == 0:
                    arrive()
                else:
                    pl.when(distance < reach)(arrive)

    def chunk_terms(k):
        i, half = lax.div(k, 2), lax.rem(k, 2)
        for stream in range(3):
            for no in range(4):
                to_partner(stream, 4 * k + no).wait_recv()
        meta = gm[pl.ds(8 * k, 8)]
        ids, route = meta[:, :8, :], meta[:, 8:, :]
        rows = 8 * CAP
        before = (
            lax.broadcasted_iota(jnp.int32, (128, 128), 0)
            < lax.broadcasted_iota(jnp.int32, (128, 128), 1)
        ).astype(F32).astype(BF16)
        row = lax.broadcasted_iota(jnp.int32, (rows, 128), 0)
        block_of = lax.shift_right_logical(row * 205, 11)
        place = (row - block_of * CAP).astype(F32)
        row8 = lax.broadcasted_iota(jnp.int32, (rows, 8), 0)
        spread = (
            lax.shift_right_logical(row8 * 205, 11)
            == lax.broadcasted_iota(jnp.int32, (rows, 8), 1)
        ).astype(F32)
        tables, weights = [], []
        for e in range(2):
            hit = ids == (2 * ex + e).astype(F32)
            sel = jnp.sum(jnp.where(hit, 1.0, 0.0), axis=1)
            weight = jnp.sum(jnp.where(hit, route, 0.0), axis=1)
            rank = dot(sel.astype(BF16), before, 1, 0)
            sel_rows = dot(spread.astype(BF16), sel.astype(BF16), 1, 0)
            rank_rows = dot(spread.astype(BF16), rank.astype(BF16), 1, 0)
            weight_rows = dot(spread, weight, 1, 0, lax.Precision.HIGHEST)
            taken = jnp.where((sel_rows > 0.5) & (rank_rows == place), 1.0, 0.0)
            weights.append(jnp.sum(taken * weight_rows, axis=1, keepdims=True))
            tables.append(
                jnp.concatenate(
                    [jnp.where(block_of == b, taken, 0.0) for b in range(8)], axis=1
                ).astype(BF16)
            )
        whole = jnp.concatenate(tables, axis=0)
        slot_weight = jnp.concatenate(weights, axis=0)
        table[k] = whole
        slot_w[k] = jnp.broadcast_to(slot_weight, (2 * rows, 128))
        picked_x = dot(whole, gx[pl.ds(8 * k, 8)].reshape(1024, -1), 1, 0).astype(BF16)
        picked_dy = (
            dot(whole, gc[pl.ds(8 * k, 8)].reshape(1024, -1), 1, 0) * slot_weight
        ).astype(BF16)
        for e in range(2):
            span = slice(rows * e, rows * (e + 1))
            pre = dot(picked_x[span], up[e], 1, 0).astype(BF16)
            slope = dot(picked_dy[span], down[e], 1, 1).astype(BF16)
            for q in range(4):
                for c in range(2):
                    lanes = slice(256 * q + 128 * c, 256 * q + 128 * (c + 1))
                    terms[i, e, q, 2 * half + c, 0] = pre[:, lanes]
                    terms[i, e, q, 2 * half + c, 1] = slope[:, lanes]

    def places(e):
        first, second = (x, y) if e == 0 else (y, x)

        def near(p):
            return lax.rem(p + 1, SIDE), lax.rem(p + 2, SIDE), lax.rem(p + 3, SIDE)

        return first, near(first), second, near(second)

    def hop(i, e, step, way, src, dst):
        axis = e if step in (0, 1, 6, 7) else 1 - e
        return remote(
            src, dst, ex_send.at[i, e, step, way], ex_recv.at[i, e, step, way],
            along(axis, 1 if way == 0 else 3),
        )

    def plus(a, b):
        return (a.astype(F32) + b.astype(F32)).astype(BF16)

    def exchange(step, i):
        for e in range(2):
            p1, (r1, o1, l1), p2, (r2, o2, l2) = places(e)
            t, s, h = terms.at[i, e], s1.at[i, e], acts.at[i, e]
            if step == 0:
                hop(i, e, 0, 0, t.at[o1, pl.ds(0, 2)], a1.at[i, e, 0]).start()
                hop(i, e, 0, 1, t.at[o1, pl.ds(2, 2)], a1.at[i, e, 1]).start()
            elif step == 1:
                for way, p in ((0, r1), (1, l1)):
                    hop(i, e, 0, way, a1.at[i, e, way], a1.at[i, e, way]).wait_recv()
                    for n in range(2):
                        m = 2 * way + n
                        terms[i, e, p, m] = plus(terms[i, e, p, m], a1[i, e, way, n])
                    hop(i, e, 1, way, t.at[p], a2.at[i, e, way]).start()
            elif step == 2:
                for way in range(2):
                    hop(i, e, 1, way, a2.at[i, e, way], a2.at[i, e, way]).wait_recv()
                for n in range(4):
                    s1[i, e, n] = (
                        terms[i, e, p1, n].astype(F32)
                        + a2[i, e, 0, n].astype(F32)
                        + a2[i, e, 1, n].astype(F32)
                    ).astype(BF16)
                for way in range(2):
                    hop(i, e, 2, way, s.at[o2, way], b1.at[i, e, way]).start()
            elif step == 3:
                for way, p in ((0, r2), (1, l2)):
                    hop(i, e, 2, way, b1.at[i, e, way], b1.at[i, e, way]).wait_recv()
                    s1[i, e, p, way] = plus(s1[i, e, p, way], b1[i, e, way])
                    hop(i, e, 3, way, s.at[p], b2.at[i, e, way]).start()
            elif step == 4:
                for way in range(2):
                    hop(i, e, 3, way, b2.at[i, e, way], b2.at[i, e, way]).wait_recv()
                total = (
                    s1[i, e, p2].astype(F32)
                    + b2[i, e, 0].astype(F32)
                    + b2[i, e, 1].astype(F32)
                )
                pre, grad_hidden = total[0], total[1]
                gate = 1.0 / (1.0 + jnp.exp(-pre))
                acts[i, e, p1, p2, 0] = (pre * gate).astype(BF16)
                acts[i, e, p1, p2, 1] = (
                    grad_hidden * (gate * (1.0 + pre * (1.0 - gate)))
                ).astype(BF16)
                for way in range(2):
                    hop(i, e, 4, way, h.at[p1, p2], h.at[p1, p2]).start()
            elif step == 5:
                for way, p in ((0, l2), (1, r2)):
                    hop(i, e, 4, way, h.at[p1, p], h.at[p1, p]).wait_recv()
                    hop(i, e, 5, way, h.at[p1, p, way], h.at[p1, p, way]).start()
            elif step == 6:
                for way in range(2):
                    hop(i, e, 5, way, h.at[p1, o2, way], h.at[p1, o2, way]).wait_recv()
                for way in range(2):
                    hop(i, e, 6, way, h.at[p1], h.at[p1]).start()
            elif step == 7:
                for way, p in ((0, l1), (1, r1)):
                    hop(i, e, 6, way, h.at[p], h.at[p]).wait_recv()
                    part = h.at[p, pl.ds(2 * way, 2)]
                    hop(i, e, 7, way, part, part).start()
            else:
                for way in range(2):
                    part = h.at[o1, pl.ds(2 * way, 2)]
                    hop(i, e, 7, way, part, part).wait_recv()

    for copy in weights_in:
        copy.wait()

    def tick(t, carry):
        pl.when(t <= reach)(lambda: gather_tick(t))

        def at(step):
            after = t - 5 - step

            @pl.when((after >= 0) & (lax.rem(after, 4) == 0) & (after < 4 * rounds))
            def _():
                exchange(step, lax.div(after, 4))

        for step in range(8, 0, -1):
            at(step)

        @pl.when((t >= 3) & (lax.rem(t, 2) == 1) & (t <= 2 * chunks + 1))
        def _():
            chunk_terms(lax.div(t - 3, 2))

        at(0)
        return carry

    lax.fori_loop(1, 4 * rounds + 10, tick, 0)

    def sent_all(no, carry):
        for stream in range(3):
            pl.when(no != own)(lambda: to_chip(stream, no, no, z_up).wait_send())
            to_partner(stream, no).wait_send()
        return carry

    lax.fori_loop(0, 2 * reach, sent_all, 0)

    def partner_share(stream, no):
        return remote(
            gathered[stream].at[2 * no + 1], pc.at[stream, no],
            back_send.at[stream, no], back_recv.at[stream, no], partner,
        )

    def running_sum(stream, no, to, device):
        return remote(
            gathered[stream].at[2 * no], rx.at[stream, to],
            rs_send.at[stream, to], rs_recv.at[stream, to], device,
        )

    def project(k):
        i, half = lax.div(k, 2), lax.rem(k, 2)
        rows = 8 * CAP
        outs, backs = [], []
        for e in range(2):
            hidden, grad_pre = (
                jnp.concatenate(
                    [acts[i, e, q, 2 * half + c, n] for q in range(4) for c in range(2)], axis=1
                )
                for n in range(2)
            )
            weight = slot_w[k, pl.ds(rows * e, rows)]
            weight = jnp.concatenate([weight] * (down.shape[2] // 128), axis=1)
            outs.append((dot(hidden, down[e], 1, 0) * weight).astype(BF16))
            backs.append(dot(grad_pre, up[e], 1, 1).astype(BF16))
        out = jnp.concatenate(outs, axis=0)
        back = jnp.concatenate(backs, axis=0)
        for b in range(8):
            chosen = table[k, :, pl.ds(128 * b, 128)]
            gx[8 * k + b] = dot(chosen, out, 0, 0).astype(BF16)
            gc[8 * k + b] = dot(chosen, back, 0, 0).astype(BF16)

    def reduce_tick(distance):
        for stream in range(2):
            g = gathered[stream]
            for way, device in ((0, z_down), (1, z_up)):
                no = pair_no(distance, way)

                def add():
                    partner_share(stream, no).wait_recv()
                    mine = g[2 * no].astype(F32) + pc[stream, no].astype(F32)
                    first = distance == reach - way

                    @pl.when(first)
                    def _():
                        g[2 * no] = mine.astype(BF16)

                    @pl.when(jnp.logical_not(first))
                    def _():
                        at = 2 * distance + way
                        running_sum(stream, no, at, device).wait_recv()
                        total = g[2 * no].astype(F32) + pc[stream, no].astype(F32)
                        g[2 * no] = (total + rx[stream, at].astype(F32)).astype(BF16)

                    running_sum(stream, no, 2 * distance - 2 + way, device).start()

                if way == 0:
                    add()
                else:
                    pl.when(distance < reach)(add)

    def back_step(n, carry):
        k = chunks - 1 - n
        project(k)
        for no in range(4):
            for stream in range(2):
                partner_share(stream, 4 * k + no).start()
        reduce_tick(2 * k + 2)
        reduce_tick(2 * k + 1)
        return carry

    lax.fori_loop(0, chunks, back_step, 0)

    for stream, out_ref in ((0, critic_ref), (1, grad_ref)):
        partner_share(stream, own).wait_recv()
        total = gathered[stream][2 * own].astype(F32) + pc[stream, own].astype(F32)
        for way, device in ((0, z_down), (1, z_up)):
            running_sum(stream, own, way, device).wait_recv()
            total = total + rx[stream, way].astype(F32)
        out_ref[...] = total.astype(BF16)

    def drain_back(no, carry):
        for stream in range(2):
            partner_share(stream, no).wait_send()
            pl.when(no < 2 * reach - 1)(
                lambda: running_sum(stream, no, no, z_up).wait_send()
            )
        return carry

    lax.fori_loop(0, 2 * reach, drain_back, 0)

    for i in range(rounds):
        for e in range(2):
            t, s, h = terms.at[i, e], s1.at[i, e], acts.at[i, e]
            sizes = (
                t.at[0, pl.ds(0, 2)], t.at[0], s.at[0, 0], s.at[0],
                h.at[0, 0], h.at[0, 0, 0], h.at[0], h.at[0, pl.ds(0, 2)],
            )
            for step in range(8):
                for way in range(2):
                    hop(i, e, step, way, sizes[step], sizes[step]).wait_send()


def solution(mesh):
    n_chips = mesh.shape["expert"] // 2
    reach = n_chips // 2
    chunks = reach // 2
    rounds = chunks // 2

    def local(tokens, cotangent, expert_ids, route_weights, up_weight, down_weight):
        count, width = tokens.shape
        units = up_weight.shape[2]
        meta = jnp.concatenate([expert_ids.T.astype(F32), route_weights.T], axis=0)
        rows = 8 * CAP
        vmem = pltpu.VMEM
        dma = pltpu.SemaphoreType.DMA
        pairs = 2 * reach
        shape = jax.ShapeDtypeStruct((count, width), BF16)
        critic_out, token_grad = pl.pallas_call(
            functools.partial(kernel, n_chips),
            out_shape=(shape, shape),
            in_specs=[pl.BlockSpec(memory_space=pltpu.VMEM)] * 3
            + [pl.BlockSpec(memory_space=pl.ANY)] * 2,
            out_specs=(pl.BlockSpec(memory_space=pltpu.VMEM),) * 2,
            scratch_shapes=[
                vmem((2, width, units), BF16),
                vmem((2, units, width), BF16),
                vmem((2 * pairs, count, width), BF16),
                vmem((2 * pairs, count, width), BF16),
                vmem((2 * pairs, 16, count), F32),
                vmem((rounds, 2, 4, 4, 2, rows, 128), BF16),
                vmem((rounds, 2, 2, 2, 2, rows, 128), BF16),
                vmem((rounds, 2, 2, 4, 2, rows, 128), BF16),
                vmem((rounds, 2, 4, 2, rows, 128), BF16),
                vmem((rounds, 2, 2, rows, 128), BF16),
                vmem((rounds, 2, 2, 2, rows, 128), BF16),
                vmem((rounds, 2, 4, 4, 2, rows, 128), BF16),
                vmem((chunks, 2 * rows, 8 * count), BF16),
                vmem((chunks, 2 * rows, 128), F32),
                vmem((2, pairs, count, width), BF16),
                vmem((2, pairs, count, width), BF16),
                dma((2,)),
                dma((3, pairs)), dma((3, pairs)), dma((3, pairs)), dma((3, pairs)),
                dma((rounds, 2, 8, 2)), dma((rounds, 2, 8, 2)),
                dma((2, pairs)), dma((2, pairs)), dma((2, pairs)), dma((2, pairs)),
            ],
            compiler_params=pltpu.CompilerParams(
                collective_id=0, has_side_effects=True, vmem_limit_bytes=62 * 1024 * 1024
            ),
        )(tokens, cotangent, meta, up_weight, down_weight)
        return critic_out, token_grad

    in_specs = (
        P("expert", "dp"),
        P("expert", "dp"),
        P("expert", None),
        P("expert", None),
        P("expert", "dp", None),
        P("expert", None, "dp"),
    )
    out_specs = (P("expert", "dp"), P("expert", "dp"))
    return jax.shard_map(local, mesh=mesh, in_specs=in_specs, out_specs=out_specs, check_vma=False)
```

time: 892 us -> 243 us (0.27); the launches traced: 881 us -> 243 us
  waiting for transfers between devices: 657 us -> 0 us
  Pallas kernels: 0 us -> 237 us
  local copies, waits for them, and re-layouts: 101 us -> 3.09 us
  starting transfers between devices: 62.9 us -> 0 us
  other arithmetic: 32 us -> 1.98 us
  between operations: 15.2 us -> 0.64 us
  matrix products: 13 us -> 0 us
    all_to_all x3 -> x0, waiting for transfers between devices: 396 us -> none  [the longest x1 185 us: local(): lax.all_to_all(returned.reshape(peers, capacity * groups, 2, width), 'exp...]
    pallas_call x0 -> x1, Pallas kernels: none -> 237 us  [local(): pl.pallas_call(functools.partial(kernel, n_chips), out_shape=(shape, shap...]
    unnamed x3 -> x0, waiting for transfers between devices: 166 us -> none
    all_gather x1 -> x0, waiting for transfers between devices: 94.7 us -> none  [local(): whole = lax.all_gather(stacked, 'dp', axis=2, tiled=True)]
    all_to_all x3 -> x0, starting transfers between devices: 62.2 us -> none  [the longest x1 30.4 us: local(): lax.all_to_all(x_send.reshape(peers, capacity * groups, width), 'expert',...]
    another operation x12 -> x0, local copies, waits for them, and re-layouts: 38.5 us -> none  [the longest x3 24 us: partial_terms(): jnp.stack([pre.reshape(-1, units), grad_hidden.reshape(-1, units)], axis=1)]
    reduce_sum x5 -> x0, other arithmetic: 21.9 us -> none  [the longest x1 9.59 us: local(): jnp.sum(match.astype(jnp.float32) * route_weights[None, :, :], axis=(1, 2))]
    all_gather x1 -> x0, local copies, waits for them, and re-layouts: 19.6 us -> none  [local(): whole = lax.all_gather(stacked, 'dp', axis=2, tiled=True)]
  transfers between devices with their start and end apart: 5 -> 0, of which waited for: 5 -> 0; matrix products, arithmetic and copies ran while one was open for 3% -> 0% of each run, Pallas kernels for 0% -> 0%
where the time goes in v1:
time: 243 us
  Pallas kernels  237 us (98%)
  local copies, waits for them, and re-layouts  3.09 us (1%)
    pallas_call x1, Pallas kernels, local(): pl.pallas_call(functools.partial(kernel, n_chips), out_shape=(shape, shap...  237 us

profile of v1, /device:TPU:1, one launch (start us, length us, event | category | flops | bytes accessed | tf_op | source)
XLA Modules:
  0.0 243.1 jit_solution(6593075427271312346)
XLA Ops:
  0.6 0.7 convert_bitcast_fusion
  1.3 1.3 pad_maximum_fusion.meta_ref
  2.6 237.4 %shard_map.77 = (bf16[128,384]{1,0:T(8,128)(2,1)}, bf16[128,384]{1,0:T(8,128)(2,1)}) custom-call(bf16[128,384]{1,0:T(8,128)(2,1)} %x_ref.1, bf16[128,384]{1,0:T(8,128)(2,1)} %dy_ref.1, f32[16,128]{1,0:T(8,128)} %pad_maximum_fusion.meta_ref, bf16[2,384,1024]{2,1,0:T(8,128)(2,1)} %up_hbm.1, bf16[2,1024,384]{2,1,0:T(8,128)(2,1)} %down_hbm.1), custom_call_target="tpu_custom_call" | custom-call | tf_op jit(solution)/shard_map/pallas_call | solution.py:401
  240.1 1.5 copy.10
  241.6 1.5 copy.11

commit v2 on v1

--- a/solution.py
+++ b/solution.py
@@ -22,8 +22,8 @@
 
 def kernel(
     n_chips,
-    x_ref, dy_ref, meta_ref, up_hbm, down_hbm, critic_ref, grad_ref,
-    up, down, gx, gc, gm, terms, a1, a2, s1, b1, b2, acts, table, slot_w, rx, pc,
+    x_ref, dy_ref, ids_ref, route_ref, up_hbm, down_hbm, critic_ref, grad_ref,
+    up, down, gx, gc, gm, terms, a1, a2, s1, b1, b2, acts, table, slot_w, picked, rx, pc,
     w_sem, ag_send, ag_recv, pair_send, pair_recv, ex_send, ex_recv,
     rs_send, rs_recv, back_send, back_recv,
 ):
@@ -66,11 +66,17 @@
 
     gathered = (gx, gc, gm)
     own = pair_no(reach, 1)
-
-    def to_chip(stream, src, dst, device):
-        g = gathered[stream]
+    part_rows = x_ref.shape[0] // 2
+
+    def piece(number, slot):
+        if number == 4:
+            return gm.at[slot]
+        return gathered[number // 2].at[slot, pl.ds(number % 2 * part_rows, part_rows)]
+
+    def to_chip(number, src, dst, device):
         return remote(
-            g.at[2 * src], g.at[2 * dst], ag_send.at[stream, dst], ag_recv.at[stream, dst], device
+            piece(number, 2 * src), piece(number, 2 * dst),
+            ag_send.at[number, dst], ag_recv.at[number, dst], device,
         )
 
     def to_partner(stream, no):
@@ -82,54 +88,64 @@
 
     gx[2 * own] = x_ref[...]
     gc[2 * own] = dy_ref[...]
-    gm[2 * own] = meta_ref[...]
-    for stream in range(3):
-        to_chip(stream, own, pair_no(1, 0), z_up).start()
-        to_chip(stream, own, pair_no(1, 1), z_down).start()
+    gm[2 * own] = jnp.concatenate([ids_ref[...].astype(F32), route_ref[...]], axis=0)
+    for number in range(5):
+        to_chip(number, own, pair_no(1, 0), z_up).start()
+        to_chip(number, own, pair_no(1, 1), z_down).start()
     for stream in range(3):
         to_partner(stream, own).start()
 
-    def gather_tick(distance):
-        for stream in range(3):
-            for way, device in ((0, z_up), (1, z_down)):
-                no = pair_no(distance, way)
-
-                def arrive():
-                    to_chip(stream, no, no, device).wait_recv()
-
-                    @pl.when(distance < reach - way)
+    def far_way(stream):
+        return 1 if stream == 1 else 0
+
+    def gather_piece(number, distance):
+        for way, device in ((0, z_up), (1, z_down)):
+            no = pair_no(distance, way)
+
+            def arrive():
+                to_chip(number, no, no, device).wait_recv()
+
+                if way == far_way(number // 2):
+
+                    @pl.when(distance < reach)
                     def _():
-                        to_chip(stream, no, no + 2, device).start()
-
-                    to_partner(stream, no).start()
-
-                if way == 0:
-                    arrive()
+                        step = 2 if way == 0 else jnp.where(distance == reach - 1, 1, 2)
+                        to_chip(number, no, no + step, device).start()
+
                 else:
-                    pl.when(distance < reach)(arrive)
-
-    def chunk_terms(k):
+
+                    @pl.when(distance < reach - 1)
+                    def _():
+                        to_chip(number, no, no + 2, device).start()
+
+                if number in (1, 3, 4):
+                    to_partner(number // 2, no).start()
+
+            pl.when(distance <= reach - way)(arrive)
+
+    def chunk_part(part, k):
         i, half = lax.div(k, 2), lax.rem(k, 2)
-        for stream in range(3):
+        rows = 8 * CAP
+        if part in (0, 2, 3):
+            stream = (2, None, 0, 1)[part]
             for no in range(4):
                 to_partner(stream, 4 * k + no).wait_recv()
-        meta = gm[pl.ds(8 * k, 8)]
-        ids, route = meta[:, :8, :], meta[:, 8:, :]
-        rows = 8 * CAP
-        before = (
-            lax.broadcasted_iota(jnp.int32, (128, 128), 0)
-            < lax.broadcasted_iota(jnp.int32, (128, 128), 1)
-        ).astype(F32).astype(BF16)
-        row = lax.broadcasted_iota(jnp.int32, (rows, 128), 0)
-        block_of = lax.shift_right_logical(row * 205, 11)
-        place = (row - block_of * CAP).astype(F32)
-        row8 = lax.broadcasted_iota(jnp.int32, (rows, 8), 0)
-        spread = (
-            lax.shift_right_logical(row8 * 205, 11)
-            == lax.broadcasted_iota(jnp.int32, (rows, 8), 1)
-        ).astype(F32)
-        tables, weights = [], []
-        for e in range(2):
+        if part < 2:
+            e = part
+            meta = gm[pl.ds(8 * k, 8)]
+            ids, route = meta[:, :8, :], meta[:, 8:, :]
+            before = (
+                lax.broadcasted_iota(jnp.int32, (128, 128), 0)
+                < lax.broadcasted_iota(jnp.int32, (128, 128), 1)
+            ).astype(F32).astype(BF16)
+            row = lax.broadcasted_iota(jnp.int32, (rows, 128), 0)
+            block_of = lax.shift_right_logical(row * 205, 11)
+            place = (row - block_of * CAP).astype(F32)
+            row8 = lax.broadcasted_iota(jnp.int32, (rows, 8), 0)
+            spread = (
+                lax.shift_right_logical(row8 * 205, 11)
+                == lax.broadcasted_iota(jnp.int32, (rows, 8), 1)
+            ).astype(F32)
             hit = ids == (2 * ex + e).astype(F32)
             sel = jnp.sum(jnp.where(hit, 1.0, 0.0), axis=1)
             weight = jnp.sum(jnp.where(hit, route, 0.0), axis=1)
@@ -138,29 +154,25 @@
             rank_rows = dot(spread.astype(BF16), rank.astype(BF16), 1, 0)
             weight_rows = dot(spread, weight, 1, 0, lax.Precision.HIGHEST)
             taken = jnp.where((sel_rows > 0.5) & (rank_rows == place), 1.0, 0.0)
-            weights.append(jnp.sum(taken * weight_rows, axis=1, keepdims=True))
-            tables.append(
-                jnp.concatenate(
-                    [jnp.where(block_of == b, taken, 0.0) for b in range(8)], axis=1
-                ).astype(BF16)
-            )
-        whole = jnp.concatenate(tables, axis=0)
-        slot_weight = jnp.concatenate(weights, axis=0)
-        table[k] = whole
-        slot_w[k] = jnp.broadcast_to(slot_weight, (2 * rows, 128))
-        picked_x = dot(whole, gx[pl.ds(8 * k, 8)].reshape(1024, -1), 1, 0).astype(BF16)
-        picked_dy = (
-            dot(whole, gc[pl.ds(8 * k, 8)].reshape(1024, -1), 1, 0) * slot_weight
-        ).astype(BF16)
-        for e in range(2):
-            span = slice(rows * e, rows * (e + 1))
-            pre = dot(picked_x[span], up[e], 1, 0).astype(BF16)
-            slope = dot(picked_dy[span], down[e], 1, 1).astype(BF16)
+            slot_weight = jnp.sum(taken * weight_rows, axis=1, keepdims=True)
+            table[k, rows * e : rows * (e + 1)] = jnp.concatenate(
+                [jnp.where(block_of == b, taken, 0.0) for b in range(8)], axis=1
+            ).astype(BF16)
+            slot_w[k, rows * e : rows * (e + 1)] = jnp.broadcast_to(slot_weight, (rows, 128))
+        elif part == 2:
+            picked[0] = dot(table[k], gx[pl.ds(8 * k, 8)].reshape(1024, -1), 1, 0).astype(BF16)
+        elif part == 3:
+            rows_dy = dot(table[k], gc[pl.ds(8 * k, 8)].reshape(1024, -1), 1, 0)
+            weight = jnp.concatenate([slot_w[k]] * (rows_dy.shape[1] // 128), axis=1)
+            picked[1] = (rows_dy * weight).astype(BF16)
+        else:
+            e, kind = (part - 4) // 2, part % 2
+            lhs = picked[kind, rows * e : rows * (e + 1)]
+            product = (dot(lhs, down[e], 1, 1) if kind else dot(lhs, up[e], 1, 0)).astype(BF16)
             for q in range(4):
                 for c in range(2):
                     lanes = slice(256 * q + 128 * c, 256 * q + 128 * (c + 1))
-                    terms[i, e, q, 2 * half + c, 0] = pre[:, lanes]
-                    terms[i, e, q, 2 * half + c, 1] = slope[:, lanes]
+                    terms[i, e, q, 2 * half + c, kind] = product[:, lanes]
 
     def places(e):
         first, second = (x, y) if e == 0 else (y, x)
@@ -249,34 +261,46 @@
         copy.wait()
 
     def tick(t, carry):
-        pl.when(t <= reach)(lambda: gather_tick(t))
-
         def at(step):
-            after = t - 5 - step
+            after = t - 6 - (0, 1, 3, 4, 5, 6, 7, 9, 10)[step]
 
             @pl.when((after >= 0) & (lax.rem(after, 4) == 0) & (after < 4 * rounds))
             def _():
                 exchange(step, lax.div(after, 4))
 
-        for step in range(8, 0, -1):
-            at(step)
-
-        @pl.when((t >= 3) & (lax.rem(t, 2) == 1) & (t <= 2 * chunks + 1))
+        odd = lax.rem(t, 2) == 1
+        for number in range(5):
+            pl.when(t <= reach)(lambda: gather_piece(number, t))
+            for step in ((8, 7), (6, 5), (4, 3), (2, 1), ())[number]:
+                at(step)
+            if number < 4:
+
+                @pl.when((t >= 3) & odd & (t <= 2 * chunks + 1))
+                def _():
+                    chunk_part(number, lax.div(t - 3, 2))
+
+                @pl.when((t >= 4) & jnp.logical_not(odd) & (t <= 2 * chunks + 2))
+                def _():
+                    chunk_part(4 + number, lax.div(t - 4, 2))
+
+        at(0)
+
+        @pl.when(t == reach + 1)
         def _():
-            chunk_terms(lax.div(t - 3, 2))
-
-        at(0)
+            lax.fori_loop(0, 2 * reach, sent_all, 0)
+
+        @pl.when((t >= reach + 4) & (t <= reach + chunks + 1))
+        def _():
+            project(t - reach - 4)
+
         return carry
 
-    lax.fori_loop(1, 4 * rounds + 10, tick, 0)
-
     def sent_all(no, carry):
+        for number in range(5):
+            pl.when(no != own)(lambda: to_chip(number, no, no, z_up).wait_send())
         for stream in range(3):
-            pl.when(no != own)(lambda: to_chip(stream, no, no, z_up).wait_send())
             to_partner(stream, no).wait_send()
         return carry
-
-    lax.fori_loop(0, 2 * reach, sent_all, 0)
 
     def partner_share(stream, no):
         return remote(
@@ -284,10 +308,11 @@
             back_send.at[stream, no], back_recv.at[stream, no], partner,
         )
 
-    def running_sum(stream, no, to, device):
+    def running_sum(number, no, to, device):
+        rows = pl.ds(number % 2 * part_rows, part_rows)
         return remote(
-            gathered[stream].at[2 * no], rx.at[stream, to],
-            rs_send.at[stream, to], rs_recv.at[stream, to], device,
+            gathered[number // 2].at[2 * no, rows], rx.at[number // 2, to, rows],
+            rs_send.at[number, to], rs_recv.at[number, to], device,
         )
 
     def project(k):
@@ -311,42 +336,50 @@
             chosen = table[k, :, pl.ds(128 * b, 128)]
             gx[8 * k + b] = dot(chosen, out, 0, 0).astype(BF16)
             gc[8 * k + b] = dot(chosen, back, 0, 0).astype(BF16)
+        for no in range(4):
+            for stream in range(2):
+                partner_share(stream, 4 * k + no).start()
+
+    lax.fori_loop(1, 4 * rounds + 13, tick, 0)
 
     def reduce_tick(distance):
-        for stream in range(2):
+        for number in range(4):
+            stream = number // 2
             g = gathered[stream]
+            rows = pl.ds(number % 2 * part_rows, part_rows)
             for way, device in ((0, z_down), (1, z_up)):
+                far = way == far_way(stream)
                 no = pair_no(distance, way)
+                if far and way == 1:
+                    no = jnp.where(distance == reach, no - 1, no)
 
                 def add():
-                    partner_share(stream, no).wait_recv()
-                    mine = g[2 * no].astype(F32) + pc[stream, no].astype(F32)
-                    first = distance == reach - way
+                    if number % 2 == 0:
+                        partner_share(stream, no).wait_recv()
+                    first = distance == (reach if far else reach - 1)
 
                     @pl.when(first)
                     def _():
-                        g[2 * no] = mine.astype(BF16)
+                        mine = g[2 * no, rows].astype(F32) + pc[stream, no, rows].astype(F32)
+                        g[2 * no, rows] = mine.astype(BF16)
 
                     @pl.when(jnp.logical_not(first))
                     def _():
                         at = 2 * distance + way
-                        running_sum(stream, no, at, device).wait_recv()
-                        total = g[2 * no].astype(F32) + pc[stream, no].astype(F32)
-                        g[2 * no] = (total + rx[stream, at].astype(F32)).astype(BF16)
-
-                    running_sum(stream, no, 2 * distance - 2 + way, device).start()
-
-                if way == 0:
+                        running_sum(number, no, at, device).wait_recv()
+                        total = g[2 * no, rows].astype(F32) + pc[stream, no, rows].astype(F32)
+                        g[2 * no, rows] = (total + rx[stream, at, rows].astype(F32)).astype(BF16)
+
+                    running_sum(number, no, 2 * distance - 2 + way, device).start()
+
+                if far:
                     add()
                 else:
                     pl.when(distance < reach)(add)
 
     def back_step(n, carry):
         k = chunks - 1 - n
-        project(k)
-        for no in range(4):
-            for stream in range(2):
-                partner_share(stream, 4 * k + no).start()
+        pl.when(n < 2)(lambda: project(k))
         reduce_tick(2 * k + 2)
         reduce_tick(2 * k + 1)
         return carry
@@ -357,16 +390,17 @@
         partner_share(stream, own).wait_recv()
         total = gathered[stream][2 * own].astype(F32) + pc[stream, own].astype(F32)
         for way, device in ((0, z_down), (1, z_up)):
-            running_sum(stream, own, way, device).wait_recv()
+            for half in range(2):
+                running_sum(2 * stream + half, own, way, device).wait_recv()
             total = total + rx[stream, way].astype(F32)
         out_ref[...] = total.astype(BF16)
 
     def drain_back(no, carry):
         for stream in range(2):
             partner_share(stream, no).wait_send()
-            pl.when(no < 2 * reach - 1)(
-                lambda: running_sum(stream, no, no, z_up).wait_send()
-            )
+        for number in range(4):
+            unused = 2 * reach - 1 - far_way(number // 2)
+            pl.when(no != unused)(lambda: running_sum(number, no, no, z_up).wait_send())
         return carry
 
     lax.fori_loop(0, 2 * reach, drain_back, 0)
@@ -392,7 +426,6 @@
     def local(tokens, cotangent, expert_ids, route_weights, up_weight, down_weight):
         count, width = tokens.shape
         units = up_weight.shape[2]
-        meta = jnp.concatenate([expert_ids.T.astype(F32), route_weights.T], axis=0)
         rows = 8 * CAP
         vmem = pltpu.VMEM
         dma = pltpu.SemaphoreType.DMA
@@ -401,7 +434,7 @@
         critic_out, token_grad = pl.pallas_call(
             functools.partial(kernel, n_chips),
             out_shape=(shape, shape),
-            in_specs=[pl.BlockSpec(memory_space=pltpu.VMEM)] * 3
+            in_specs=[pl.BlockSpec(memory_space=pltpu.VMEM)] * 4
             + [pl.BlockSpec(memory_space=pl.ANY)] * 2,
             out_specs=(pl.BlockSpec(memory_space=pltpu.VMEM),) * 2,
             scratch_shapes=[
@@ -419,17 +452,18 @@
                 vmem((rounds, 2, 4, 4, 2, rows, 128), BF16),
                 vmem((chunks, 2 * rows, 8 * count), BF16),
                 vmem((chunks, 2 * rows, 128), F32),
+                vmem((2, 2 * rows, width), BF16),
                 vmem((2, pairs, count, width), BF16),
                 vmem((2, pairs, count, width), BF16),
                 dma((2,)),
-                dma((3, pairs)), dma((3, pairs)), dma((3, pairs)), dma((3, pairs)),
+                dma((5, pairs)), dma((5, pairs)), dma((3, pairs)), dma((3, pairs)),
                 dma((rounds, 2, 8, 2)), dma((rounds, 2, 8, 2)),
-                dma((2, pairs)), dma((2, pairs)), dma((2, pairs)), dma((2, pairs)),
+                dma((4, pairs)), dma((4, pairs)), dma((2, pairs)), dma((2, pairs)),
             ],
             compiler_params=pltpu.CompilerParams(
                 collective_id=0, has_side_effects=True, vmem_limit_bytes=62 * 1024 * 1024
             ),
-        )(tokens, cotangent, meta, up_weight, down_weight)
+        )(tokens, cotangent, expert_ids.T, route_weights.T, up_weight, down_weight)
         return critic_out, token_grad
 
     in_specs = (

time: 243 us -> 227 us (0.934)
  Pallas kernels: 237 us -> 223 us
    pallas_call x1, Pallas kernels: 237 us -> 223 us  [local(): pl.pallas_call(functools.partial(kernel, n_chips), out_shape=(shape, shap...]
where the time goes in v2:
time: 227 us
  Pallas kernels  223 us (98%)
  local copies, waits for them, and re-layouts  3.09 us (1%)
    pallas_call x1, Pallas kernels, local(): pl.pallas_call(functools.partial(kernel, n_chips), out_shape=(shape, shap...  223 us

profile of v2, /device:TPU:1, one launch (start us, length us, event | category | flops | bytes accessed | tf_op | source)
XLA Modules:
  0.0 226.6 jit_solution(17071043709610869371)
XLA Ops:
  0.6 222.9 %shard_map.77 = (bf16[128,384]{1,0:T(8,128)(2,1)}, bf16[128,384]{1,0:T(8,128)(2,1)}) custom-call(bf16[128,384]{1,0:T(8,128)(2,1)} %x_ref.1, bf16[128,384]{1,0:T(8,128)(2,1)} %dy_ref.1, s32[8,128]{1,0:T(8,128)} %bitcast.2, f32[8,128]{1,0:T(8,128)} %bitcast.3, bf16[2,384,1024]{2,1,0:T(8,128)(2,1)} %up_hbm.1, bf16[2,1024,384]{2,1,0:T(8,128)(2,1)} %down_hbm.1), custom_call_target="tpu_custom_call" | custom-call | tf_op jit(solution)/shard_map/pallas_call | solution.py:434
  223.5 1.5 copy.10
  225.1 1.5 copy.11
